TPU v7x, 256 devices: a whole 4x4x8 slice. The times are simulated.
256 devices in a mesh: row: 64 (over z, x, core), col: 4 (over y).
Axes of the slice: x: 4, y: 4, z: 8, core: 2. Of those that a mesh axis runs over, the one named last changes fastest.
Arguments:
- student_states: bfloat16 [16384, 4096], P('row', 'col'), may hold values from -24 to 24
- student_proj: bfloat16 [2048, 4096], P('row', 'col'), may hold values from -0.09375 to 0.09375
- teacher_states: bfloat16 [1024, 4096], P('col', 'row'), may hold values from -6 to 6
- teacher_proj: bfloat16 [2048, 4096], P('col', 'row'), may hold values from -0.09375 to 0.09375
Outputs:
- grad_student: float32 [2048, 4096], P('row', 'col')
- grad_teacher: float32 [2048, 4096], P('col', 'row')
All inputs are finite; a program needn't handle non-finite values.
Results may differ from a plain program's by a relative error of at most 0.014.
The roundings to bfloat16 on the way count: a program that leaves them out, or rounds other values in their place, can miss the bound.
Values may be sent and summed in bfloat16 or wider, within the bound.
A program may use at most 64 MiB of HBM per device.

v0:
```python
import math

import jax
import jax.numpy as jnp
from jax import lax
from jax.sharding import PartitionSpec as P

E = 2048
ITERS = 3
S_DEV = 256
T_DEV = 256


TEMPER = 50.0
RIGHT_CONTRACT = (((1,), (1,)), ((), ()))
LEFT_CONTRACT = (((0,), (0,)), ((), ()))


def row_lse(values):
    local_max = jnp.max(values, axis=1)
    maxima = lax.pmax(local_max, "col")
    totals = lax.psum(jnp.sum(jnp.exp(values - maxima[:, None]), axis=1), "col")
    return maxima + jnp.log(totals)


def col_lse(values):
    local_max = jnp.max(values, axis=0)
    maxima = lax.pmax(local_max, "row")
    totals = lax.psum(jnp.sum(jnp.exp(values - maxima[None, :]), axis=0), "row")
    return maxima + jnp.log(totals)


def col_sums(values):
    return lax.psum(jnp.sum(values, axis=0), "row")


def row_sums(values):
    return lax.psum(jnp.sum(values, axis=1), "col")


def per_device(student_states, student_proj, teacher_states, teacher_proj):
    partial_student = lax.dot_general(
        student_states,
        lax.all_gather(student_proj, "row", axis=0, tiled=True),
        RIGHT_CONTRACT,
        preferred_element_type=jnp.float32,
    )
    student_emb = lax.psum(partial_student, "col").astype(jnp.bfloat16)
    teacher_full = lax.all_gather(teacher_proj, "col", axis=0, tiled=True)
    partial_teacher = lax.dot_general(
        teacher_states, teacher_full, RIGHT_CONTRACT, preferred_element_type=jnp.float32
    )
    teacher_emb = lax.psum(partial_teacher, "row").astype(jnp.bfloat16)
    norm_student = jnp.sum(jnp.square(student_emb.astype(jnp.float32)), axis=1)
    norm_teacher = jnp.sum(jnp.square(teacher_emb.astype(jnp.float32)), axis=1)
    inverse_temp = TEMPER / E
    cross = lax.dot_general(
        student_emb, teacher_emb, RIGHT_CONTRACT, preferred_element_type=jnp.float32
    )
    logits = inverse_temp * (2.0 * cross - norm_student[:, None] - norm_teacher[None, :])
    col_pots = [jnp.zeros((teacher_emb.shape[0],), jnp.float32)]
    row_pots = []
    for sweep in range(ITERS):
        row_pot = -row_lse(logits + col_pots[-1][None, :])
        row_pots.append(row_pot)
        col_pots.append(-col_lse(logits + row_pot[:, None]))
    weight = math.sqrt(S_DEV * lax.axis_size("row")) / (T_DEV * lax.axis_size("col"))
    plan = jnp.exp(logits + row_pots[-1][:, None] + col_pots[-1][None, :])
    loss_term = -weight * plan * logits
    col_grad = col_sums(loss_term)
    adjoint = loss_term - weight * plan - plan * col_grad[None, :]
    row_grad = row_sums(loss_term - plan * col_grad[None, :])
    for sweep in range(ITERS - 1, -1, -1):
        flow_term = (
            jnp.exp(logits + row_pots[sweep][:, None] + col_pots[sweep][None, :])
            * row_grad[:, None]
        )
        adjoint = adjoint - flow_term
        if sweep > 0:
            col_grad = -col_sums(flow_term)
            back_term = (
                jnp.exp(logits + row_pots[sweep - 1][:, None] + col_pots[sweep][None, :])
                * col_grad[None, :]
            )
            adjoint = adjoint - back_term
            row_grad = -row_sums(back_term)
    adjoint_low = adjoint.astype(jnp.bfloat16)
    student_part = (
        2.0
        * inverse_temp
        * (
            jnp.dot(adjoint_low, teacher_emb, preferred_element_type=jnp.float32)
            - jnp.sum(adjoint, axis=1)[:, None] * student_emb.astype(jnp.float32)
        )
    )
    student_adj = lax.psum(student_part, "col").astype(jnp.bfloat16)
    columns = student_adj
    grad_student = lax.psum_scatter(
        lax.dot_general(columns, student_states, LEFT_CONTRACT, preferred_element_type=jnp.float32),
        "row",
        scatter_dimension=0,
        tiled=True,
    )
    col_mass = jnp.sum(adjoint, axis=0)
    columns = adjoint_low
    product = lax.dot_general(
        columns, student_emb, LEFT_CONTRACT, preferred_element_type=jnp.float32
    )
    teacher_share = lax.psum_scatter(
        2.0 * inverse_temp * (product - col_mass[:, None] * teacher_emb.astype(jnp.float32)),
        "row",
        scatter_dimension=0,
        tiled=True,
    )
    teacher_adj = lax.all_gather(teacher_share.astype(jnp.bfloat16), "row", axis=0, tiled=True)
    columns = teacher_adj
    grad_teacher = lax.psum_scatter(
        lax.dot_general(
            columns, teacher_states, LEFT_CONTRACT, preferred_element_type=jnp.float32
        ).astype(jnp.bfloat16),
        "col",
        scatter_dimension=0,
        tiled=True,
    ).astype(jnp.float32)
    return (grad_student, grad_teacher)


def solution(mesh):
    placed = (P("row", "col"), P("row", "col"), P("col", "row"), P("col", "row"))
    return jax.shard_map(
        per_device,
        mesh=mesh,
        in_specs=placed,
        out_specs=(P("row", "col"), P("col", "row")),
        check_vma=False,
    )
```

profile of v0, /device:TPU:8, one launch (start us, length us, event | category | flops | bytes accessed | tf_op | source)
XLA Modules:
  0.0 2095.2 jit_solution(4511180237447404467)
XLA Ops:
  7.2 0.0 all-gather.4.cloned.1.call-start
  7.2 0.7 all-gather.4.cloned.1.call-update
  7.9 0.0 all-gather.6.cloned.1.call-start
  8.0 12.7 all_gather.10
  20.7 2.5 fusion.20
  23.3 0.6 dynamic-slice
  24.5 273.0 %all-reduce.6 = bf16[256,2048]{1,0:T(8,128)(2,1)S(1)} all-reduce(f32[256,2048]{1,0:T(8,128)} %fusion.20), channel_id=1, replica_groups=mesh['row'=64,'col'=4] {'row'}, use_global_device_ids=true, to_apply=%region_1.0 | all-reduce | flops 524288 | bytes 3145728 | tf_op jit(solution)/shard_map/psum | solution.py:53
  297.5 0.3 fusion.3
  297.8 0.0 all-gather.4.cloned.1.call-done
  297.8 4.8 fusion.19
  302.6 39.6 %all-reduce.5 = bf16[256,2048]{1,0:T(8,128)(2,1)S(1)} all-reduce(f32[256,2048]{1,0:T(8,128)} %fusion.19), channel_id=1, replica_groups=mesh['row'=64,'col'=4] {'col'}, use_global_device_ids=true, to_apply=%region_0.0 | all-reduce | flops 524288 | bytes 3145728 | tf_op jit(solution)/shard_map/psum | solution.py:48
  342.2 0.3 fusion.2
  342.5 0.6 fusion.18
  343.1 9.2 pmax.42
  352.2 0.2 exponential_reduce_fusion.5
  352.4 9.5 psum.107
  362.0 0.1 add_reduce_fusion.2
  362.1 124.1 %pmax.43 = f32[256]{0:T(256)S(1)} all-reduce(f32[256]{0:T(256)S(1)} %add_reduce_fusion.2), channel_id=1, replica_groups=mesh['row'=64,'col'=4] {'row'}, use_global_device_ids=true, to_apply=%region_9.0 | all-reduce | flops 256 | bytes 2048 | tf_op jit(solution)/shard_map/pmax | solution.py:28
  486.1 0.1 exponential_reduce_fusion.4
  486.3 124.1 %psum.108 = f32[256]{0:T(256)S(1)} all-reduce(f32[256]{0:T(256)S(1)} %exponential_reduce_fusion.4), channel_id=1, replica_groups=mesh['row'=64,'col'=4] {'row'}, use_global_device_ids=true, to_apply=%region_11.0 | all-reduce | flops 256 | bytes 2048 | tf_op jit(solution)/shard_map/psum | solution.py:29
  610.3 0.1 add_reduce_fusion.1
  610.5 8.0 pmax.44
  618.4 0.2 exponential_reduce_fusion.3
  618.6 9.5 psum.109
  628.1 0.1 add_reduce_fusion.4
  628.3 124.1 %pmax.45 = f32[256]{0:T(256)S(1)} all-reduce(f32[256]{0:T(256)S(1)} %add_reduce_fusion.4), channel_id=1, replica_groups=mesh['row'=64,'col'=4] {'row'}, use_global_device_ids=true, to_apply=%region_17.0 | all-reduce | flops 256 | bytes 2048 | tf_op jit(solution)/shard_map/pmax | solution.py:28
  752.3 0.1 exponential_reduce_fusion.2
  752.5 124.1 %psum.110 = f32[256]{0:T(256)S(1)} all-reduce(f32[256]{0:T(256)S(1)} %exponential_reduce_fusion.2), channel_id=1, replica_groups=mesh['row'=64,'col'=4] {'row'}, use_global_device_ids=true, to_apply=%region_19.0 | all-reduce | flops 256 | bytes 2048 | tf_op jit(solution)/shard_map/psum | solution.py:29
  876.5 0.1 add_reduce_fusion
  876.6 8.0 pmax.46
  884.6 0.2 exponential_reduce_fusion.1
  884.8 9.5 psum.111
  894.3 0.1 add_reduce_fusion.3
  894.5 124.1 %pmax.47 = f32[256]{0:T(256)S(1)} all-reduce(f32[256]{0:T(256)S(1)} %add_reduce_fusion.3), channel_id=1, replica_groups=mesh['row'=64,'col'=4] {'row'}, use_global_device_ids=true, to_apply=%region_25.0 | all-reduce | flops 256 | bytes 2048 | tf_op jit(solution)/shard_map/pmax | solution.py:28
  1018.5 0.1 exponential_reduce_fusion
  1018.6 124.1 %psum.112 = f32[256]{0:T(256)S(1)} all-reduce(f32[256]{0:T(256)S(1)} %exponential_reduce_fusion), channel_id=1, replica_groups=mesh['row'=64,'col'=4] {'row'}, use_global_device_ids=true, to_apply=%region_27.0 | all-reduce | flops 256 | bytes 2048 | tf_op jit(solution)/shard_map/psum | solution.py:29
  1142.7 0.2 fusion.13
  1142.9 124.1 %psum.113 = f32[256]{0:T(256)S(1)} all-reduce(f32[256]{0:T(256)S(1)} %fusion.13), channel_id=1, replica_groups=mesh['row'=64,'col'=4] {'row'}, use_global_device_ids=true, to_apply=%region_29.0 | all-reduce | flops 256 | bytes 2048 | tf_op jit(solution)/shard_map/psum | solution.py:34
  1266.9 0.2 subtract_reduce_fusion
  1267.1 8.0 psum.114
  1275.1 0.2 fusion.10
  1275.3 124.1 %psum.115 = f32[256]{0:T(256)S(1)} all-reduce(f32[256]{0:T(256)S(1)} %fusion.10), channel_id=1, replica_groups=mesh['row'=64,'col'=4] {'row'}, use_global_device_ids=true, to_apply=%region_33.0 | all-reduce | flops 256 | bytes 2048 | tf_op jit(solution)/shard_map/psum | solution.py:34
  1399.3 0.2 fusion.11
  1399.5 9.5 psum.116
  1409.1 0.1 fusion.12
  1409.2 124.1 %psum.117 = f32[256]{0:T(256)S(1)} all-reduce(f32[256]{0:T(256)S(1)} %fusion.12), channel_id=1, replica_groups=mesh['row'=64,'col'=4] {'row'}, use_global_device_ids=true, to_apply=%region_37.0 | all-reduce | flops 256 | bytes 2048 | tf_op jit(solution)/shard_map/psum | solution.py:34
  1533.3 0.2 fusion.9
  1533.5 8.0 psum.118
  1541.4 0.5 fusion.17
  1541.9 1.8 fusion
  1543.8 267.7 %all-reduce.8 = bf16[256,2048]{1,0:T(8,128)(2,1)} all-reduce(f32[256,2048]{1,0:T(8,128)} %fusion), channel_id=3, replica_groups=mesh['row'=64,'col'=4] {'row'}, use_global_device_ids=true, to_apply=%region_44.0.clone | all-reduce | flops 524288 | bytes 3145728
  1811.5 1.4 fusion.16
  1812.9 0.0 reduce-scatter.5.cloned.1.call-start
  1813.0 1.8 fusion.1
  1814.8 69.8 %all-gather.6.cloned.1.call-done = bf16[64,4,2048]{2,1,0:T(4,128)(2,1)} async-done(((bf16[1,4,2048]{2,1,0:T(4,128)(2,1)}), bf16[64,4,2048]{2,1,0:T(4,128)(2,1)}) %all-gather.6.cloned.1.call-update) | async-done | bytes 1048592 | tf_op jit(solution)/shard_map/all_gather | solution.py:115
  1884.5 2.1 reshape.27
  1886.7 2.2 convolution_convert_fusion
  1888.9 0.0 reduce-scatter.3.cloned.1.call-start
  1889.0 44.7 %all-reduce.7 = bf16[256,2048]{1,0:T(8,128)(2,1)} all-reduce(f32[256,2048]{1,0:T(8,128)S(1)} %copy-done.1), channel_id=1, replica_groups=mesh['row'=64,'col'=4] {'col'}, use_global_device_ids=true, to_apply=%region_41.0 | all-reduce | flops 524288 | bytes 3145728 | tf_op jit(solution)/shard_map/psum | solution.py:96
  1933.7 5.7 fusion.21
  1939.5 0.0 reduce-scatter.3.cloned.1.call-update
  1939.5 0.0 reduce-scatter.5.cloned.1.call-done
  1939.5 1.5 convert_element_type.37
  1941.0 147.7 %reduce-scatter.3.cloned.1.call-done = f32[32,1024]{1,0:T(8,128)} async-done(((f32[2048,1024]{1,0:T(8,128)}), f32[32,1024]{1,0:T(8,128)}) %reduce-scatter.3.cloned.1.call-update) | async-done | bytes 131088 | tf_op jit(solution)/shard_map/reduce_scatter | solution.py:98
  (20 shorter events, 0.1 us)
Async XLA Ops:
  7.2 290.6 %copy-start = (bf16[256,1024]{1,0:T(8,128)(2,1)S(1)}, bf16[256,1024]{1,0:T(8,128)(2,1)}, u32[]{:S(2)}) copy-start(bf16[256,1024]{1,0:T(8,128)(2,1)} %param.4) | copy-start | bytes 1572868
  7.2 16.1 copy-start.3
  7.2 290.6 %all-gather.4.cloned.1.call-start = ((), (), s32[]{:S(2)}) async-start(), calls=%async_computation.2 | async-start | bytes 4259840 | tf_op jit(solution)/shard_map/all_gather | solution.py:44
  7.9 1876.6 %all-gather.6.cloned.1.call-start = ((), (), s32[]{:S(2)}) async-start(), calls=%async_computation.5 | async-start | bytes 1064960 | tf_op jit(solution)/shard_map/all_gather | solution.py:115
  1812.9 126.6 %reduce-scatter.5.cloned.1.call-start = ((), (), s32[]{:S(2)}) async-start(), calls=%async_computation.4 | async-start | bytes 327680 | tf_op jit(solution)/shard_map/reduce_scatter | solution.py:117
  1813.0 73.7 %copy-start.2 = (bf16[256,64]{0,1:T(8,128)(2,1)S(1)}, bf16[256,64]{0,1:T(8,128)(2,1)}, u32[]{:S(2)}) copy-start(bf16[256,64]{0,1:T(8,128)(2,1)} %param.6) | copy-start | bytes 98308
  1814.8 74.2 %copy-start.1 = (f32[256,2048]{1,0:T(8,128)S(1)}, f32[256,2048]{1,0:T(8,128)}, u32[]{:S(2)}) copy-start(f32[256,2048]{1,0:T(8,128)} %fusion.1) | copy-start | bytes 6291460
  1888.9 199.8 %reduce-scatter.3.cloned.1.call-start = ((), (), s32[]{:S(2)}) async-start(), calls=%async_computation.3 | async-start | bytes 8519680 | tf_op jit(solution)/shard_map/reduce_scatter | solution.py:98
Sparse Core Ops, SparseCore 0:
  10.8 81.8 all-gather.3
  1813.0 71.4 all-gather.5
  1889.1 19.9 reduce-scatter.4
  1939.6 149.0 reduce-scatter.2
where the time goes:
time: 2100 us
  blocking collectives  1830 us (87%)
  waiting for transfers between devices  218 us (10%)
    psum x3, blocking collectives, col_lse(): totals = lax.psum(jnp.sum(jnp.exp(values - maxima[None, :]), axis=0), 'row')  372 us
    psum x3, blocking collectives, col_sums(): return lax.psum(jnp.sum(values, axis=0), 'row')  372 us
    pmax x3, blocking collectives, col_lse(): maxima = lax.pmax(local_max, 'row')  372 us
    psum x1, blocking collectives, per_device(): teacher_emb = lax.psum(partial_teacher, 'row').astype(jnp.bfloat16)  273 us
    unnamed x1, blocking collectives  268 us
    reduce_scatter x1, waiting for transfers between devices, per_device(): lax.psum_scatter(lax.dot_general(columns, student_states, LEFT_CONTRACT,...  148 us
    all_gather x1, waiting for transfers between devices, per_device(): lax.all_gather(teacher_share.astype(jnp.bfloat16), 'row', axis=0, tiled=T...  69.8 us
    psum x1, blocking collectives, per_device(): student_adj = lax.psum(student_part, 'col').astype(jnp.bfloat16)  44.7 us
  transfers between devices with their start and end apart: 4, of which 2 were waited for; matrix products, arithmetic and copies ran while one was open for 1% of the time, Pallas kernels for 0%

commit v1 on v0

v1 whole, which is shorter than its diff:
```python
import math

import jax
import jax.numpy as jnp
from jax import lax
from jax.experimental import pallas as pl
from jax.experimental.pallas import tpu as pltpu
from jax.sharding import PartitionSpec as P

MESH = pl.DeviceIdType.MESH
WEIGHT = math.sqrt(16384) / 1024


def coords():
    r = lax.axis_index("row")
    y = lax.axis_index("col")
    c = lax.rem(r, 2)
    x = lax.rem(r // 2, 4)
    z = r // 8
    return x, y, z, c


def dev(x, y, z, c):
    return ((z * 4 + x) * 2 + c, y)


def partner(stage, i, pos):
    x, y, z, c = pos
    if stage == 0:
        q = lax.rem(x * 4 + y + i, 16)
        return dev(q // 4, lax.rem(q, 4), z, c), q
    q = lax.rem(z * 2 + c + i, 16)
    return dev(x, y, q // 2, lax.rem(q, 2)), q


def sink_kernel(logits_ref, adj_ref, sbuf, rbuf, send_sem, recv_sem):
    pos = coords()
    x, y, z, c = pos
    mine = (x * 4 + y, z * 2 + c)
    barrier = pltpu.get_barrier_semaphore()

    for stage in range(2):
        def greet(i, carry):
            target, _ = partner(stage, i, pos)
            pl.semaphore_signal(barrier, inc=1, device_id=target, device_id_type=MESH)
            return carry
        lax.fori_loop(1, 16, greet, 0)
    pl.semaphore_wait(barrier, 30)

    def start(k, stage, n):
        def body(i, carry):
            target, _ = partner(stage, i, pos)
            pltpu.make_async_remote_copy(
                src_ref=sbuf.at[k, stage, pl.ds(0, n)],
                dst_ref=rbuf.at[k, stage, mine[stage], pl.ds(0, n)],
                send_sem=send_sem.at[k, stage],
                recv_sem=recv_sem.at[k, stage],
                device_id=target,
                device_id_type=MESH,
            ).start()
            return carry
        lax.fori_loop(1, 16, body, 0)

    def arrive(k, stage, n):
        ref = rbuf.at[k, stage, pl.ds(0, 15), pl.ds(0, n)]
        pltpu.make_async_copy(ref, ref, recv_sem.at[k, stage]).wait()

    def pack(k, stage, q, row):
        for j in range(8):
            sbuf[k, stage, q, pl.ds(j, 1), :] = row[:, j * 128:(j + 1) * 128]

    def unpack(k, q):
        return jnp.concatenate([sbuf[k, 2, q, pl.ds(j, 1), :] for j in range(8)], axis=1)

    def reduce_sum(k, row):
        pack(k, 0, 0, row)
        for stage in range(2):
            start(k, stage, 1)
            rbuf[k, stage, mine[stage], 0] = sbuf[k, stage, 0]
            arrive(k, stage, 1)
            sbuf[k, stage + 1, 0] = jnp.sum(rbuf[k, stage, :, 0], axis=0)
        return unpack(k, 0)

    def reduce_lse(k, top, total):
        pack(k, 0, 0, top)
        pack(k, 0, 1, total)
        for stage in range(2):
            start(k, stage, 2)
            rbuf[k, stage, mine[stage], pl.ds(0, 2)] = sbuf[k, stage, pl.ds(0, 2)]
            arrive(k, stage, 2)
            tops = rbuf[k, stage, :, 0]
            best = jnp.max(tops, axis=0)
            sbuf[k, stage + 1, 0] = best
            sbuf[k, stage + 1, 1] = jnp.sum(
                rbuf[k, stage, :, 1] * jnp.exp(tops - best[None]), axis=0)
        sbuf[k, 2, 0] = -(sbuf[k, 2, 0] + jnp.log(sbuf[k, 2, 1]))
        return unpack(k, 0)

    def reduce_last(k, top, total, moment):
        pack(k, 0, 0, top)
        pack(k, 0, 1, total)
        pack(k, 0, 2, moment)
        for stage in range(2):
            start(k, stage, 3)
            rbuf[k, stage, mine[stage]] = sbuf[k, stage]
            arrive(k, stage, 3)
            tops = rbuf[k, stage, :, 0]
            best = jnp.max(tops, axis=0)
            scale = jnp.exp(tops - best[None])
            sbuf[k, stage + 1, 0] = best
            sbuf[k, stage + 1, 1] = jnp.sum(rbuf[k, stage, :, 1] * scale, axis=0)
            sbuf[k, stage + 1, 2] = jnp.sum(rbuf[k, stage, :, 2] * scale, axis=0)
        sbuf[k, 2, 0] = -(sbuf[k, 2, 0] + jnp.log(sbuf[k, 2, 1]))
        sbuf[k, 2, 2] = -WEIGHT * sbuf[k, 2, 2] / sbuf[k, 2, 1]
        return unpack(k, 0), unpack(k, 2)

    logits = logits_ref[...]
    gs = [None]
    fs = [None]
    for k in range(3):
        v = logits if gs[k] is None else logits + gs[k]
        top = jnp.max(v, axis=1, keepdims=True)
        f = -(top + jnp.log(jnp.sum(jnp.exp(v - top), axis=1, keepdims=True)))
        fs.append(f)
        v = logits + f
        top = jnp.max(v, axis=0, keepdims=True)
        e = jnp.exp(v - top)
        total = jnp.sum(e, axis=0, keepdims=True)
        if k < 2:
            gs.append(reduce_lse(k, top, total))
        else:
            moment = jnp.sum(e * logits, axis=0, keepdims=True)
            g, gbar = reduce_last(k, top, total, moment)
            gs.append(g)
    plan = jnp.exp(logits + fs[3] + gs[3])
    loss = -WEIGHT * plan * logits
    adjoint = loss - WEIGHT * plan - plan * gbar
    fbar = jnp.sum(loss - plan * gbar, axis=1, keepdims=True)
    for k in (3, 2, 1):
        v = logits + fs[k]
        if k > 1:
            v = v + gs[k - 1]
        flow = jnp.exp(v) * fbar
        adjoint = adjoint - flow
        if k > 1:
            gbar = -reduce_sum(6 - k, jnp.sum(flow, axis=0, keepdims=True))
            flow2 = jnp.exp(logits + fs[k - 1] + gs[k - 1]) * gbar
            adjoint = adjoint - flow2
            fbar = -jnp.sum(flow2, axis=1, keepdims=True)
    adj_ref[...] = adjoint
    for stage in range(2):
        for k, n in enumerate((2, 2, 3, 1, 1)):
            ref = rbuf.at[k, stage, pl.ds(0, 15), pl.ds(0, n)]
            pltpu.make_async_copy(ref, ref, send_sem.at[k, stage]).wait()


def sinkhorn(logits):
    return pl.pallas_call(
        sink_kernel,
        out_shape=jax.ShapeDtypeStruct((64, 1024), jnp.float32),
        in_specs=[pl.BlockSpec(memory_space=pltpu.VMEM)],
        out_specs=pl.BlockSpec(memory_space=pltpu.VMEM),
        scratch_shapes=[
            pltpu.VMEM((5, 3, 3, 8, 128), jnp.float32),
            pltpu.VMEM((5, 2, 16, 3, 8, 128), jnp.float32),
            pltpu.SemaphoreType.DMA((5, 2)),
            pltpu.SemaphoreType.DMA((5, 2)),
        ],
        compiler_params=pltpu.CompilerParams(
            collective_id=0, has_side_effects=True, vmem_limit_bytes=32 * 2**20),
        name="sinkhorn",
    )(logits)


RIGHT_CONTRACT = (((1,), (1,)), ((), ()))
LEFT_CONTRACT = (((0,), (0,)), ((), ()))
INVERSE_TEMP = 50.0 / 2048


def per_device(student_states, student_proj, teacher_states, teacher_proj):
    partial_student = lax.dot_general(
        student_states,
        lax.all_gather(student_proj, "row", axis=0, tiled=True),
        RIGHT_CONTRACT,
        preferred_element_type=jnp.float32,
    )
    emb = lax.psum(partial_student, "col").astype(jnp.bfloat16)
    teacher_full = lax.all_gather(teacher_proj, "col", axis=0, tiled=True)
    partial_teacher = lax.dot_general(
        teacher_states, teacher_full, RIGHT_CONTRACT, preferred_element_type=jnp.float32
    )
    teacher_part = lax.psum(partial_teacher, "row").astype(jnp.bfloat16)
    teacher_emb = lax.all_gather(teacher_part, "col", axis=0, tiled=True)
    col = lax.axis_index("col")
    student_emb = lax.dynamic_slice_in_dim(emb, col * 64, 64, 0)
    norm_student = jnp.sum(jnp.square(student_emb.astype(jnp.float32)), axis=1)
    norm_teacher = jnp.sum(jnp.square(teacher_emb.astype(jnp.float32)), axis=1)
    cross = lax.dot_general(
        student_emb, teacher_emb, RIGHT_CONTRACT, preferred_element_type=jnp.float32
    )
    logits = INVERSE_TEMP * (2.0 * cross - norm_student[:, None] - norm_teacher[None, :])
    adjoint = sinkhorn(logits)
    adjoint_low = adjoint.astype(jnp.bfloat16)
    student_adj = (
        2.0
        * INVERSE_TEMP
        * (
            jnp.dot(adjoint_low, teacher_emb, preferred_element_type=jnp.float32)
            - jnp.sum(adjoint, axis=1)[:, None] * student_emb.astype(jnp.float32)
        )
    ).astype(jnp.bfloat16)
    columns = lax.all_gather(student_adj, "col", axis=0, tiled=True)
    grad_student = lax.psum_scatter(
        lax.dot_general(columns, student_states, LEFT_CONTRACT, preferred_element_type=jnp.float32),
        "row",
        scatter_dimension=0,
        tiled=True,
    )
    adjoint_rows = lax.all_to_all(adjoint, "col", split_axis=1, concat_axis=0, tiled=True)
    col_mass = jnp.sum(adjoint_rows, axis=0)
    product = lax.dot_general(
        adjoint_rows.astype(jnp.bfloat16), emb, LEFT_CONTRACT, preferred_element_type=jnp.float32
    )
    teacher_share = lax.psum_scatter(
        2.0 * INVERSE_TEMP * (product - col_mass[:, None] * teacher_part.astype(jnp.float32)),
        "row",
        scatter_dimension=0,
        tiled=True,
    )
    teacher_adj = lax.all_gather(teacher_share.astype(jnp.bfloat16), "row", axis=0, tiled=True)
    grad_teacher = lax.psum_scatter(
        lax.dot_general(
            teacher_adj, teacher_states, LEFT_CONTRACT, preferred_element_type=jnp.float32
        ).astype(jnp.bfloat16),
        "col",
        scatter_dimension=0,
        tiled=True,
    ).astype(jnp.float32)
    return (grad_student, grad_teacher)


def solution(mesh):
    placed = (P("row", "col"), P("row", "col"), P("col", "row"), P("col", "row"))
    return jax.shard_map(
        per_device,
        mesh=mesh,
        in_specs=placed,
        out_specs=(P("row", "col"), P("col", "row")),
        check_vma=False,
    )
```

time: 2100 us -> 1100 us (0.52)
  blocking collectives: 1830 us -> 596 us
  waiting for transfers between devices: 218 us -> 397 us
  Pallas kernels: 0 us -> 60.5 us
    psum x15 -> x2, blocking collectives: 1160 us -> 315 us  [the longest x1 272 us: per_device(): teacher_part = lax.psum(partial_teacher, 'row').astype(jnp.bfloat16)]
    pmax x6 -> x0, blocking collectives: 397 us -> none  [the longest x3 372 us: col_lse(): maxima = lax.pmax(local_max, 'row')]
    all_gather x1, waiting for transfers between devices: 0.02 us -> 79.7 us  [per_device(): lax.all_gather(student_proj, 'row', axis=0, tiled=True)]
    all_gather x0 -> x2, waiting for transfers between devices: none -> 67.7 us  [the longest x1 45.1 us: per_device(): teacher_emb = lax.all_gather(teacher_part, 'col', axis=0, tiled=True)]
    pallas_call x0 -> x1, Pallas kernels: none -> 60.5 us  [sinkhorn(): pl.pallas_call(sink_kernel, out_shape=jax.ShapeDtypeStruct((64, 1024), jn...]
  transfers between devices with their start and end apart: 4 -> 7, of which waited for: 2 -> 7; matrix products, arithmetic and copies ran while one was open for 1% -> 2% of each run, Pallas kernels for 0% -> 0%
where the time goes in v1:
time: 1100 us
  blocking collectives  596 us (54%)
  waiting for transfers between devices  397 us (36%)
  Pallas kernels  60.5 us (6%)
  matrix products  22.1 us (2%)
  between operations  14.8 us (1%)
    psum x1, blocking collectives, per_device(): teacher_part = lax.psum(partial_teacher, 'row').astype(jnp.bfloat16)  272 us
    unnamed x1, blocking collectives  268 us
    reduce_scatter x1, waiting for transfers between devices, per_device(): lax.psum_scatter(lax.dot_general(columns, student_states, LEFT_CONTRACT,...  157 us
    all_gather x1, waiting for transfers between devices, per_device(): lax.all_gather(student_proj, 'row', axis=0, tiled=True)  79.7 us
    all_gather x1, waiting for transfers between devices, per_device(): lax.all_gather(teacher_share.astype(jnp.bfloat16), 'row', axis=0, tiled=T...  68.2 us
    pallas_call x1, Pallas kernels, sinkhorn(): pl.pallas_call(sink_kernel, out_shape=jax.ShapeDtypeStruct((64, 1024), jn...  60.5 us
    all_gather x1, waiting for transfers between devices, per_device(): teacher_emb = lax.all_gather(teacher_part, 'col', axis=0, tiled=True)  45.1 us
    psum x1, blocking collectives, per_device(): emb = lax.psum(partial_student, 'col').astype(jnp.bfloat16)  43 us
  transfers between devices with their start and end apart: 7, of which 7 were waited for; matrix products, arithmetic and copies ran while one was open for 2% of the time, Pallas kernels for 0%

profile of v1, /device:TPU:8, one launch (start us, length us, event | category | flops | bytes accessed | tf_op | source)
XLA Modules:
  0.0 1103.1 jit_solution(13064154407887806007)
XLA Ops:
  7.2 0.0 copy-start
  7.2 0.0 all-gather.8.cloned.1.call-start
  7.2 12.9 %all_gather.16 = bf16[2048,64]{0,1:T(8,128)(2,1)S(1)} all-gather(bf16[512,64]{0,1:T(8,128)(2,1)} %param.7), channel_id=1, replica_groups=mesh['row'=64,'col'=4] {'col'}, dimensions={0}, use_global_device_ids=true | all-gather | bytes 327680 | tf_op jit(solution)/shard_map/all_gather | solution.py:188
  20.1 1.2 fusion.13
  21.3 271.8 %all-reduce.5 = bf16[256,2048]{1,0:T(8,128)(2,1)} all-reduce(f32[256,2048]{1,0:T(8,128)S(1)} %fusion.13), channel_id=1, replica_groups=mesh['row'=64,'col'=4] {'row'}, use_global_device_ids=true, to_apply=%region_1.0 | all-reduce | flops 524288 | bytes 3145728 | tf_op jit(solution)/shard_map/psum | solution.py:192
  293.1 0.0 all-gather.8.cloned.1.call-update
  293.1 0.0 all-gather.6.cloned.1.call-start
  293.2 0.7 all-gather.6.cloned.1.call-update
  293.9 45.1 %all-gather.8.cloned.1.call-done = bf16[1024,2048]{1,0:T(8,128)(2,1)} async-done(((bf16[256,2048]{1,0:T(8,128)(2,1)}), bf16[1024,2048]{1,0:T(8,128)(2,1)}) %all-gather.8.cloned.1.call-update) | async-done | bytes 4194320 | tf_op jit(solution)/shard_map/all_gather | solution.py:193
  339.0 3.1 multiply_reduce_fusion
  342.0 79.7 %all-gather.6.cloned.1.call-done = bf16[2048,1024]{1,0:T(8,128)(2,1)} async-done(((bf16[32,1024]{1,0:T(8,128)(2,1)}), bf16[2048,1024]{1,0:T(8,128)(2,1)}) %all-gather.6.cloned.1.call-update) | async-done | bytes 4194320 | tf_op jit(solution)/shard_map/all_gather | solution.py:183
  421.7 0.0 copy-done
  421.7 4.9 fusion.12
  426.6 0.0 copy-start.3
  426.6 43.0 %all-reduce.4 = bf16[256,2048]{1,0:T(8,128)(2,1)S(1)} all-reduce(f32[256,2048]{1,0:T(8,128)} %fusion.12), channel_id=1, replica_groups=mesh['row'=64,'col'=4] {'col'}, use_global_device_ids=true, to_apply=%region_0.0 | all-reduce | flops 524288 | bytes 3145728 | tf_op jit(solution)/shard_map/psum | solution.py:187
  469.6 0.0 copy-start.1
  469.6 0.2 fusion.6
  469.8 3.7 fusion.5.logits_ref
  473.5 60.5 %sinkhorn.1 = f32[64,1024]{1,0:T(8,128)S(1)} custom-call(f32[64,1024]{1,0:T(8,128)S(1)} %fusion.5.logits_ref), custom_call_target="tpu_custom_call" | custom-call | tf_op jit(solution)/shard_map/sinkhorn/pallas_call | solution.py:158
  534.0 0.7 copy.10
  534.7 4.8 all-to-all-start
  539.5 0.0 all-gather.12.cloned.1.call-start
  539.5 0.0 copy-done.3
  539.5 0.6 dynamic-slice
  540.7 4.4 all-to-all-done
  545.1 0.0 copy-done.1
  545.2 1.8 fusion
  547.0 268.3 %all-reduce.6 = bf16[256,2048]{1,0:T(8,128)(2,1)S(1)} all-reduce(f32[256,2048]{1,0:T(8,128)} %fusion), channel_id=3, replica_groups=mesh['row'=64,'col'=4] {'row'}, use_global_device_ids=true, to_apply=%region_7.0.clone | all-reduce | flops 524288 | bytes 3145728
  815.2 0.0 copy-start.2
  815.3 0.6 fusion.9
  815.9 0.0 all-gather.12.cloned.1.call-update
  815.9 0.0 all-gather.10.cloned.1.call-start
  816.0 0.1 reduce_sum.38
  816.1 3.8 fusion.2
  819.8 0.0 all-gather.10.cloned.1.call-update
  819.9 0.0 reduce-scatter.5.cloned.1.call-start
  819.9 68.2 %all-gather.12.cloned.1.call-done = bf16[64,4,2048]{2,1,0:T(4,128)(2,1)} async-done(((bf16[1,4,2048]{2,1,0:T(4,128)(2,1)}), bf16[64,4,2048]{2,1,0:T(4,128)(2,1)}) %all-gather.12.cloned.1.call-update) | async-done | bytes 1048592 | tf_op jit(solution)/shard_map/all_gather | solution.py:230
  888.1 1.3 reshape.13
  889.4 0.0 copy-done.2
  889.4 1.0 convolution_convert_fusion
  890.4 0.0 reduce-scatter.5.cloned.1.call-update
  890.5 0.0 reduce-scatter.3.cloned.1.call-start
  890.5 22.6 %all-gather.10.cloned.1.call-done = bf16[256,2048]{1,0:T(8,128)(2,1)} async-done(((bf16[64,2048]{1,0:T(8,128)(2,1)}), bf16[256,2048]{1,0:T(8,128)(2,1)}) %all-gather.10.cloned.1.call-update) | async-done | bytes 1048592 | tf_op jit(solution)/shard_map/all_gather | solution.py:212
  913.1 5.7 fusion.14
  918.9 0.0 reduce-scatter.3.cloned.1.call-update
  918.9 19.2 %reduce-scatter.5.cloned.1.call-done = bf16[512,64]{0,1:T(8,128)(2,1)} async-done(((bf16[2048,64]{0,1:T(8,128)(2,1)}), bf16[512,64]{0,1:T(8,128)(2,1)}) %reduce-scatter.5.cloned.1.call-update) | async-done | bytes 65552 | tf_op jit(solution)/shard_map/reduce_scatter | solution.py:231
  938.1 1.5 convert_element_type.52
  939.6 156.6 %reduce-scatter.3.cloned.1.call-done = f32[32,1024]{1,0:T(8,128)} async-done(((f32[2048,1024]{1,0:T(8,128)}), f32[32,1024]{1,0:T(8,128)}) %reduce-scatter.3.cloned.1.call-update) | async-done | bytes 131088 | tf_op jit(solution)/shard_map/reduce_scatter | solution.py:213
  (1 shorter events, 0.0 us)
Async XLA Ops:
  7.2 414.6 %copy-start = (bf16[256,1024]{1,0:T(8,128)(2,1)S(1)}, bf16[256,1024]{1,0:T(8,128)(2,1)}, u32[]{:S(2)}) copy-start(bf16[256,1024]{1,0:T(8,128)(2,1)} %param.4) | copy-start | bytes 1572868
  7.2 331.8 %all-gather.8.cloned.1.call-start = ((), (), s32[]{:S(2)}) async-start(), calls=%async_computation.4 | async-start | bytes 5242880 | tf_op jit(solution)/shard_map/all_gather | solution.py:193
  293.1 128.6 %all-gather.6.cloned.1.call-start = ((), (), s32[]{:S(2)}) async-start(), calls=%async_computation.3 | async-start | bytes 4259840 | tf_op jit(solution)/shard_map/all_gather | solution.py:183
  426.6 112.9 %copy-start.3 = (u32[256]{0:T(256)S(1)}, u32[256]{0:T(256)}, u32[]{:S(2)}) copy-start(u32[256]{0:T(256)} %constant.22) | copy-start | bytes 3076
  469.6 75.5 %copy-start.1 = (bf16[256,2048]{1,0:T(8,128)(2,1)S(1)}, bf16[256,2048]{1,0:T(8,128)(2,1)}, u32[]{:S(2)}) copy-start(bf16[256,2048]{1,0:T(8,128)(2,1)} %all-reduce.5) | copy-start | bytes 3145732
  534.7 10.4 all-to-all-start
  539.5 348.6 %all-gather.12.cloned.1.call-start = ((), (), s32[]{:S(2)}) async-start(), calls=%async_computation.8 | async-start | bytes 1064960 | tf_op jit(solution)/shard_map/all_gather | solution.py:230
  815.2 74.2 %copy-start.2 = (bf16[256,64]{0,1:T(8,128)(2,1)S(1)}, bf16[256,64]{0,1:T(8,128)(2,1)}, u32[]{:S(2)}) copy-start(bf16[256,64]{0,1:T(8,128)(2,1)} %param.6) | copy-start | bytes 98308
  815.9 97.2 %all-gather.10.cloned.1.call-start = ((), (), s32[]{:S(2)}) async-start(), calls=%async_computation.5 | async-start | bytes 1310720 | tf_op jit(solution)/shard_map/all_gather | solution.py:212
  819.9 118.2 %reduce-scatter.5.cloned.1.call-start = ((), (), s32[]{:S(2)}) async-start(), calls=%async_computation.7 | async-start | bytes 327680 | tf_op jit(solution)/shard_map/reduce_scatter | solution.py:231
  890.5 205.8 %reduce-scatter.3.cloned.1.call-start = ((), (), s32[]{:S(2)}) async-start(), calls=%async_computation.6 | async-start | bytes 8519680 | tf_op jit(solution)/shard_map/reduce_scatter | solution.py:213
Sparse Core Ops, SparseCore 0:
  293.3 45.6 all-gather.7
  341.7 79.9 all-gather.5
  816.0 71.9 all-gather.11
  889.7 23.3 all-gather.9
  915.5 22.5 reduce-scatter.4
  943.3 152.8 reduce-scatter.2
